TPU v7x, 1024 devices: a whole 8x8x8 slice. The times are simulated.
1024 devices in a mesh: node: 32 (over x_lo, y, core), local: 32 (over x_hi, z).
Axes of the slice: x: 8 (x_hi: 4, x_lo: 2; x = x_hi * 2 + x_lo), y: 8, z: 8, core: 2. Of those that a mesh axis runs over, the one named last changes fastest.
Arguments:
- context: bfloat16 [393216, 768], P(('node', 'local')), may hold values from -6 to 6
- cotangent: bfloat16 [393216, 1536], P(('node', 'local')), may hold values from -24 to 24
- weight_codes: bfloat16 [768, 1536], P('local', 'node'), may hold values from -0.21875 to 0.21875
- scales: bfloat16 [768, 32], P('local', 'node'), may hold values from 0.5 to 2
- lengths: int32 [1024], P(('node', 'local')), may hold values from 96 to 384, as said below
Outputs:
- encoded: bfloat16 [393216, 1536], P(('node', 'local'))
- ctx_grad: bfloat16 [393216, 768], P(('node', 'local'))
- weight_grad: float32 [768, 1536], P('local', 'node')
Inputs may be any that keep to these rules, and one draw needn't show every extreme that they name: `lengths`: rows of an utterance past its length are padding. Some utterance has all 384 frames in every draw.
All inputs are finite; a program needn't handle non-finite values.
Results may differ from a plain program's by a relative error of at most 0.005.
Values may be sent and summed in bfloat16 or wider, within the bound.
A program may use at most 64 MiB of HBM per device.

v0:
```python
import jax
import jax.numpy as jnp
from jax import lax
from jax.sharding import PartitionSpec as P

QBLOCK = 48


def body(context, cotangent, weight_codes, scales, lengths):
    frames = context.shape[0]
    samples = lax.axis_size("node") * lax.axis_size("local")
    usable = (jnp.arange(frames, dtype=jnp.int32) < lengths[0])[:, None]
    masked = jnp.where(usable, cotangent, jnp.zeros_like(cotangent))
    pulled_codes, pulled_scales = (
        lax.all_gather(weight_codes, "node", axis=1, tiled=True),
        lax.all_gather(scales, "node", axis=1, tiled=True),
    )
    own_rows = pulled_codes.shape[0]
    secondary = (
        (
            pulled_codes.astype(jnp.float32).reshape(own_rows, -1, QBLOCK)
            * pulled_scales.astype(jnp.float32)[:, :, None]
        )
        .reshape(own_rows, -1)
        .astype(jnp.bfloat16)
    )
    columns = context
    product = jnp.dot(
        columns,
        lax.all_gather(secondary, "local", axis=0, tiled=True),
        preferred_element_type=jnp.float32,
    )
    ctx_grad = lax.dot_general(
        masked,
        lax.all_gather(secondary, "local", axis=0, tiled=True),
        (((1,), (1,)), ((), ())),
        preferred_element_type=jnp.float32,
    )
    encoded = jnp.where(usable, product, jnp.zeros_like(product)).astype(jnp.bfloat16)
    ctx_grad = ctx_grad.astype(jnp.bfloat16)
    factor = 1.0 / samples
    columns = context
    partial_sum = lax.psum_scatter(
        lax.dot_general(
            columns, masked, (((0,), (0,)), ((), ())), preferred_element_type=jnp.float32
        )
        * factor,
        "local",
        scatter_dimension=0,
        tiled=True,
    )
    weight_grad = lax.psum_scatter(partial_sum, "node", scatter_dimension=1, tiled=True)
    return (encoded, ctx_grad, weight_grad)


def solution(mesh):
    return jax.shard_map(
        body,
        mesh=mesh,
        in_specs=(
            P(("node", "local"), None),
            P(("node", "local"), None),
            P("local", "node"),
            P("local", "node"),
            P(("node", "local")),
        ),
        out_specs=(P(("node", "local"), None), P(("node", "local"), None), P("local", "node")),
        check_vma=False,
    )
```

profile of v0, /device:TPU:1, one launch (start us, length us, event | category | flops | bytes accessed | tf_op | source)
XLA Modules:
  0.0 549.1 jit_solution(13473603548311158156)
XLA Ops:
  7.2 0.0 copy-start
  7.2 0.0 copy-start.1
  7.2 0.0 all-gather.4.cloned.1.call-start
  7.2 44.5 %all-gather.1 = bf16[32,1,24]{2,1,0:T(2,128)(2,1)S(1)} all-gather(bf16[1,1,24]{2,1,0:T(2,128)(2,1)} %bitcast.26), channel_id=1, replica_groups=mesh['node'=32,'local'=32] {'node'}, dimensions={0}, use_global_device_ids=true | all-gather | bytes 1584 | tf_op jit(solution)/shard_map/all_gather | solution.py:16
  51.8 0.1 copy.15
  51.8 33.0 %all-gather = bf16[32,48,24]{1,2,0:T(8,128)(2,1)S(1)} all-gather(bf16[1,48,24]{1,2,0:T(8,128)(2,1)} %bitcast.25), channel_id=1, replica_groups=mesh['node'=32,'local'=32] {'node'}, dimensions={0}, use_global_device_ids=true | all-gather | bytes 76032 | tf_op jit(solution)/shard_map/all_gather | solution.py:15
  84.9 0.2 reshape.20
  85.1 0.2 mul.20
  85.3 0.2 mul.21
  85.5 0.7 fusion.2
  86.2 0.0 all-gather.4.cloned.1.call-update
  86.2 0.0 reduce-scatter.7.cloned.1.call-start
  86.9 0.0 copy-done
  86.9 0.0 copy-done.1
  86.9 3.7 multiply_bitcast_fusion
  90.6 6.1 %copy.18 = f32[768,1536]{1,0:T(8,128)} copy(f32[768,1536]{0,1:T(8,128)} %multiply_bitcast_fusion) | data formatting | bytes 9437184
  96.6 0.0 reduce-scatter.7.cloned.1.call-update
  96.7 0.0 reduce-scatter.5.cloned.1.call-start
  96.7 78.4 %all-gather.4.cloned.1.call-done = bf16[768,1536]{1,0:T(8,128)(2,1)} async-done(((bf16[24,1536]{1,0:T(8,128)(2,1)}), bf16[768,1536]{1,0:T(8,128)(2,1)}) %all-gather.4.cloned.1.call-update) | async-done | bytes 2359312 | tf_op jit(solution)/shard_map/all_gather | solution.py:30
  175.1 3.1 fusion.1
  178.2 1.5 copy.16
  179.7 237.7 %reduce-scatter.7.cloned.1.call-done = f32[24,1536]{1,0:T(8,128)} async-done(((f32[768,1536]{1,0:T(8,128)}), f32[24,1536]{1,0:T(8,128)}) %reduce-scatter.7.cloned.1.call-update) | async-done | bytes 147472
  417.4 2.1 copy.19
  419.5 0.0 reduce-scatter.5.cloned.1.call-update
  419.5 3.6 convolution_convert_fusion
  423.1 118.1 %reduce-scatter.5.cloned.1.call-done = f32[24,48]{0,1:T(8,128)} async-done(((f32[24,1536]{0,1:T(8,128)}), f32[24,48]{0,1:T(8,128)}) %reduce-scatter.5.cloned.1.call-update) | async-done | bytes 4624 | tf_op jit(solution)/shard_map/reduce_scatter | solution.py:52
  541.2 1.4 copy.17
  (3 shorter events, 0.1 us)
Async XLA Ops:
  7.2 79.7 %copy-start = (bf16[384,768]{1,0:T(8,128)(2,1)S(1)}, bf16[384,768]{1,0:T(8,128)(2,1)}, u32[]{:S(2)}) copy-start(bf16[384,768]{1,0:T(8,128)(2,1)} %param.5) | copy-start | bytes 1769476
  7.2 79.7 %copy-start.1 = (bf16[384,1536]{1,0:T(8,128)(2,1)S(1)}, bf16[384,1536]{1,0:T(8,128)(2,1)}, u32[]{:S(2)}) copy-start(bf16[384,1536]{1,0:T(8,128)(2,1)} %param.6) | copy-start | bytes 3538948
  7.2 167.9 %all-gather.4.cloned.1.call-start = ((), (), s32[]{:S(2)}) async-start(), calls=%async_computation.2 | async-start | bytes 2433024 | tf_op jit(solution)/shard_map/all_gather | solution.py:30
  86.2 331.2 %reduce-scatter.7.cloned.1.call-start = ((), (), s32[]{:S(2)}) async-start(), calls=%async_computation.4 | async-start | bytes 4866048
  96.7 444.5 %reduce-scatter.5.cloned.1.call-start = ((), (), s32[]{:S(2)}) async-start(), calls=%async_computation.3 | async-start | bytes 811008 | tf_op jit(solution)/shard_map/reduce_scatter | solution.py:52
Sparse Core Ops, SparseCore 0:
  86.3 88.7 all-gather.3
  180.8 236.5 reduce-scatter.6
  420.8 120.3 reduce-scatter.4
where the time goes:
time: 550 us; the launch traced here: 549 us
  waiting for transfers between devices  434 us (79%)
  blocking collectives  77.6 us (14%)
  between operations  14.5 us (3%)
  local copies, waits for them, and re-layouts  11.7 us (2%)
  matrix products  10.4 us (2%)
    unnamed x4, waiting for transfers between devices  238 us
    reduce_scatter x1, waiting for transfers between devices, body(): lax.psum_scatter(partial_sum, 'node', scatter_dimension=1, tiled=True)  118 us
    all_gather x1, waiting for transfers between devices, body(): lax.all_gather(secondary, 'local', axis=0, tiled=True)  78.4 us
    all_gather x1, blocking collectives, body(): lax.all_gather(scales, 'node', axis=1, tiled=True)  44.5 us
    all_gather x1, blocking collectives, body(): lax.all_gather(weight_codes, 'node', axis=1, tiled=True)  33 us
    unnamed x8, local copies, waits for them, and re-layouts  11 us
  transfers between devices with their start and end apart: 3, of which 3 were waited for; matrix products, arithmetic and copies ran while one was open for 3% of the time, Pallas kernels for 0%

commit v1 on v0

v1 whole, which is shorter than its diff:
```python
import jax
import jax.numpy as jnp
from jax import lax
from jax.experimental import pallas as pl
from jax.experimental.pallas import tpu as pltpu
from jax.sharding import PartitionSpec as P

MESH = pl.DeviceIdType.MESH
F32, BF16 = jnp.float32, jnp.bfloat16
N = 8
AGQ = 4
RIGHT, LEFT = 0, 1


def kernel(
    context_hbm, cotangent_hbm, codes_ref, scales_ref, lengths_ref,
    encoded_ref, ctx_grad_ref, weight_grad_ref,
    context, cotangent, grad, grad_in, weight, block,
    zsend, zbuf, ypack, ysend, ybuf,
    ring_out, ring_in, rsend, rbuf, xsend, xbuf,
    load_sem, z_s, z_r, y_s, y_r, ag_s, ag_r, fw_s, fw_r,
    pair_s, pair_r, ring_s, ring_r, ry_s, ry_r, rx_s, rx_r,
):
    node, local = lax.axis_index("node"), lax.axis_index("local")
    core, y, x_lo = node % 2, (node // 2) % N, node // (2 * N)
    x_hi, z = local // N, local % N
    x = x_hi * 2 + x_lo

    def at(cx, cy, cz, cc):
        return (((cx % 2) * N + cy) * 2 + cc, (cx // 2) * N + cz)

    def copy(src, dst, send, recv, target):
        return pltpu.make_async_remote_copy(
            src_ref=src, dst_ref=dst, send_sem=send, recv_sem=recv,
            device_id=target, device_id_type=MESH,
        )

    me, mate = at(x, y, z, core), at(x, y, z, 1 - core)

    load_ctx = pltpu.make_async_copy(context_hbm, context, load_sem.at[0])
    load_cot = pltpu.make_async_copy(cotangent_hbm, cotangent, load_sem.at[1])
    load_ctx.start()
    load_cot.start()
    barrier = pltpu.get_barrier_semaphore()

    def greet(target):
        pl.semaphore_signal(barrier, inc=1, device_id=target, device_id_type=MESH)

    greet(mate)
    for k in range(1, N):
        greet(at(x, y, (z + k) % N, core))
        for cc in range(2):
            greet(at(x, (y + k) % N, z, cc))
            greet(at((x + k) % N, y, z, cc))

    own = (codes_ref[...].astype(F32) * scales_ref[...].astype(F32)).astype(BF16)
    zsend[0:24, 0:48] = own

    usable = lax.broadcasted_iota(jnp.int32, (context.shape[0], 1), 0) < lengths_ref[0]
    load_ctx.wait()
    context[...] = jnp.where(usable, context[...], jnp.zeros_like(context))
    load_cot.wait()
    for i in range(2):
        for h in range(2):
            part = lax.dot_general(
                context[:, i * 384 : (i + 1) * 384], cotangent[:, h * 768 : (h + 1) * 768],
                (((0,), (0,)), ((), ())), preferred_element_type=F32,
            )
            grad[h, 2 * i : 2 * i + 2] = part.reshape(2, N, 24, 768)

    pl.semaphore_wait(barrier, 1 + 5 * (N - 1))

    z_copies = [
        copy(zsend, zbuf.at[z], z_s.at[k], z_r.at[z], at(x, y, (z + k) % N, core))
        for k in range(1, N)
    ]
    for c in z_copies:
        c.start()
    zbuf[z] = zsend[...]

    order = (4, 3, 5, 2, 6, 1, 7, 0)
    pair = {}
    for k in order:
        seg = (z + k) % N
        pair[k] = copy(
            grad.at[1 - core, :, seg], grad_in.at[k], pair_s.at[k], pair_r.at[k], mate
        )
        pair[k].start()

    paired = set()

    def own_part(k, q):
        if k not in paired:
            pair[k].wait_recv()
            paired.add(k)
        h, j = q // 2, q % 2
        cols = slice(j * 384, (j + 1) * 384)
        mine = grad[core, 2 * h : 2 * h + 2, (z + k) % N, :, cols]
        return (mine + grad_in[k, 2 * h : 2 * h + 2, :, cols]).reshape(48, 384)

    zn = (at(x, y, (z + 1) % N, core), at(x, y, (z + N - 1) % N, core))
    ring = {}

    def ring_send(way, d, q):
        k = d if way == RIGHT else N - d
        part = own_part(k, q)
        if (way, d + 1, q) in ring:
            ring[way, d + 1, q].wait_recv()
            part = part + ring_in[way, d + 1, q].astype(F32)
        ring_out[way, d, q] = part.astype(BF16)
        c = copy(
            ring_out.at[way, d, q], ring_in.at[way, d, q], ring_s.at[way, d, q],
            ring_r.at[way, d, q], zn[way],
        )
        c.start()
        ring[way, d, q] = c

    def ring_step(d):
        for q in range(4):
            for way in (RIGHT, LEFT):
                if d == 4 and (q < 2) != (way == RIGHT):
                    continue
                ring_send(way, d, q)

    ring_step(4)
    for q in (2, 3):
        ring_send(RIGHT, 3, q)
    for q in (0, 1):
        ring_send(LEFT, 3, q)

    for k in range(1, N):
        s = (z + k) % N
        copy(zbuf.at[s], zbuf.at[s], z_s.at[k], z_r.at[s], me).wait_recv()
    for s in range(N):
        row, lane = (s % 4) * 24, (s // 4) * 64
        ypack[row : row + 24, lane : lane + 48] = zbuf[s, 0:24, 0:48].astype(F32)
    ysend[...] = ypack[...].astype(BF16)
    taker = y // 4
    slot = (y % 4) * 2 + core
    y_copies = [
        copy(ysend, ybuf.at[slot], y_s.at[k], y_r.at[slot], at(x, (y + k) % N, z, taker))
        for k in range(N)
    ]
    for c in y_copies[1:]:
        c.start()

    @pl.when(taker != core)
    def _():
        y_copies[0].start()

    @pl.when(taker == core)
    def _():
        ybuf[slot] = ysend[...]

    for q in (0, 1):
        ring_send(RIGHT, 3, q)
    for q in (2, 3):
        ring_send(LEFT, 3, q)
    ring_step(2)

    for s in range(N):
        @pl.when((4 * core + s // 2 != y) | (core != s % 2))
        def _():
            copy(ybuf.at[s], ybuf.at[s], y_s.at[0], y_r.at[s], me).wait_recv()

        block[0:96, s * 48 : (s + 1) * 48] = ybuf[s, :, 0:48].astype(F32)
        block[96:192, s * 48 : (s + 1) * 48] = ybuf[s, :, 64:112].astype(F32)

    rows = 192 // AGQ

    def place(k, q):
        cx = (x + k) % N
        row = pl.multiple_of((cx // 2) * 192 + q * rows, 16)
        col = pl.multiple_of((cx % 2) * 768 + core * 384, 128)
        return weight.at[pl.ds(row, rows), pl.ds(col, 384)]

    for q in range(AGQ):
        place(0, q)[...] = block[q * rows : (q + 1) * rows, :].astype(BF16)

    xn = (at((x + 1) % N, y, z, core), at((x + N - 1) % N, y, z, core))
    gather, forward = {}, []

    def gather_send(way, s, q):
        if s > 1:
            gather[way, s - 1, q].wait_recv()
        k = 1 - s if way == RIGHT else s - 1
        if s <= 3 or (q < AGQ // 2) == (way == RIGHT):
            spot = place(k + N, q)
            c = copy(spot, spot, ag_s.at[way, s, q], ag_r.at[way, s, q], xn[way])
            c.start()
            gather[way, s, q] = c
        if s > 1 or way == RIGHT:
            share(way, s - 1, q)

    def share(way, s, q):
        k = -s if way == RIGHT else s
        spot = place(k + N, q)
        c = copy(spot, spot, fw_s.at[way, s, q], fw_r.at[way, s, q], mate)
        c.start()
        forward.append((way, s, q))

    def gather_step(s):
        for q in range(AGQ):
            for way in (RIGHT, LEFT):
                gather_send(way, s, q)

    gather_step(1)
    ring_step(1)
    gather_step(2)

    total = []
    for q in range(4):
        a, b = (1, 1)
        ring[RIGHT, a, q].wait_recv()
        ring[LEFT, b, q].wait_recv()
        total.append(
            own_part(0, q) + ring_in[RIGHT, a, q].astype(F32) + ring_in[LEFT, b, q].astype(F32)
        )
    for h in range(2):
        for k in range(N):
            j, lane = k // 4, (k % 4) * 96
            rsend[k, h * 48 : (h + 1) * 48, 0:96] = total[2 * h + j][:, lane : lane + 96].astype(BF16)
    ry_copies = [
        copy(rsend.at[(y + k) % N], rbuf.at[y], ry_s.at[k], ry_r.at[y], at(x, (y + k) % N, z, core))
        for k in range(1, N)
    ]
    for c in ry_copies:
        c.start()

    gather_step(3)

    summed = rsend[y].astype(F32)
    for k in range(1, N):
        s = (y + k) % N
        copy(rbuf.at[s], rbuf.at[s], ry_s.at[k], ry_r.at[s], me).wait_recv()
        summed = summed + rbuf[s].astype(F32)
    for i in range(4):
        for cc in range(2):
            xsend[i, cc, :, 0:48] = summed[i * 24 : (i + 1) * 24, cc * 48 : (cc + 1) * 48]
    rx_copies = []
    for k in range(4):
        for e in range(2):
            i, cc = (x_hi + k) % 4, (core + e) % 2
            rx_copies.append(copy(
                xsend.at[i, cc], xbuf.at[x], rx_s.at[2 * k + e], rx_r.at[x], at(i * 2 + core, y, z, cc)
            ))
    for c in rx_copies[1:]:
        c.start()

    @pl.when(x_lo != core)
    def _():
        rx_copies[0].start()

    @pl.when(x_lo == core)
    def _():
        xbuf[x] = xsend[x_hi, core]

    gather_step(4)
    for q in range(AGQ):
        way = RIGHT if q < AGQ // 2 else LEFT
        gather[way, 4, q].wait_recv()
        share(way, 4, q)

    for k in range(1, N):
        s = (x + k) % N
        copy(xbuf.at[s], xbuf.at[s], rx_s.at[0], rx_r.at[s], me).wait_recv()

    @pl.when(x_lo != core)
    def _():
        copy(xbuf.at[x], xbuf.at[x], rx_s.at[0], rx_r.at[x], me).wait_recv()

    last = xbuf[0]
    for s in range(1, N):
        last = last + xbuf[s]
    weight_grad_ref[...] = last[:, 0:48] * (1.0 / 1024)

    for way, s, q in forward:
        k = -s if way == RIGHT else s
        cx = (x + k + N) % N
        row = pl.multiple_of((cx // 2) * 192 + q * rows, 16)
        col = pl.multiple_of((cx % 2) * 768 + (1 - core) * 384, 128)
        spot = weight.at[pl.ds(row, rows), pl.ds(col, 384)]
        copy(spot, spot, fw_s.at[way, s, q], fw_r.at[way, s, q], mate).wait_recv()

    for j in range(4):
        cols = slice(j * 384, (j + 1) * 384)
        encoded_ref[:, cols] = jnp.dot(
            context[...], weight[:, cols], preferred_element_type=F32
        ).astype(BF16)
    for j in range(2):
        cols = slice(j * 384, (j + 1) * 384)
        product = lax.dot_general(
            cotangent[...], weight[cols, :], (((1,), (1,)), ((), ())), preferred_element_type=F32
        )
        ctx_grad_ref[:, cols] = jnp.where(usable, product, jnp.zeros_like(product)).astype(BF16)

    for c in z_copies + y_copies[1:] + ry_copies + rx_copies[1:]:
        c.wait_send()

    @pl.when(taker != core)
    def _():
        y_copies[0].wait_send()

    @pl.when(x_lo != core)
    def _():
        rx_copies[0].wait_send()

    for c in list(pair.values()) + list(ring.values()) + list(gather.values()):
        c.wait_send()
    for way, s, q in forward:
        spot = place((-s if way == RIGHT else s) + N, q)
        copy(spot, spot, fw_s.at[way, s, q], fw_r.at[way, s, q], mate).wait_send()


def body(context, cotangent, codes, scales, lengths):
    frames, hrows = context.shape
    width = cotangent.shape[1]
    vmem = pl.BlockSpec(memory_space=pltpu.VMEM)
    hbm = pl.BlockSpec(memory_space=pl.ANY)
    dma = pltpu.SemaphoreType.DMA
    return pl.pallas_call(
        kernel,
        out_shape=(
            jax.ShapeDtypeStruct((frames, width), BF16),
            jax.ShapeDtypeStruct((frames, hrows), BF16),
            jax.ShapeDtypeStruct(codes.shape, F32),
        ),
        in_specs=[hbm, hbm, vmem, vmem, pl.BlockSpec(memory_space=pltpu.SMEM)],
        out_specs=(vmem, vmem, vmem),
        scratch_shapes=[
            pltpu.VMEM((frames, hrows), BF16),
            pltpu.VMEM((frames, width), BF16),
            pltpu.VMEM((2, 4, N, 24, width // 2), F32),
            pltpu.VMEM((N, 4, 24, width // 2), F32),
            pltpu.VMEM((hrows, width), BF16),
            pltpu.VMEM((192, 384), F32),
            pltpu.VMEM((32, 128), BF16),
            pltpu.VMEM((N, 32, 128), BF16),
            pltpu.VMEM((96, 128), F32),
            pltpu.VMEM((96, 128), BF16),
            pltpu.VMEM((N, 96, 128), BF16),
            pltpu.VMEM((2, 5, 4, 48, 384), BF16),
            pltpu.VMEM((2, 5, 4, 48, 384), BF16),
            pltpu.VMEM((N, 96, 128), BF16),
            pltpu.VMEM((N, 96, 128), BF16),
            pltpu.VMEM((4, 2, 24, 128), F32),
            pltpu.VMEM((N, 24, 128), F32),
            dma((2,)),
            dma((N,)), dma((N,)),
            dma((N,)), dma((N,)),
            dma((2, 5, AGQ)), dma((2, 5, AGQ)),
            dma((2, 5, AGQ)), dma((2, 5, AGQ)),
            dma((N,)), dma((N,)),
            dma((2, 5, 4)), dma((2, 5, 4)),
            dma((N,)), dma((N,)),
            dma((N,)), dma((N,)),
        ],
        compiler_params=pltpu.CompilerParams(
            collective_id=0, has_side_effects=True, vmem_limit_bytes=48 * 2**20
        ),
    )(context, cotangent, codes, scales, lengths)


def solution(mesh):
    return jax.shard_map(
        body,
        mesh=mesh,
        in_specs=(
            P(("node", "local"), None),
            P(("node", "local"), None),
            P("local", "node"),
            P("local", "node"),
            P(("node", "local")),
        ),
        out_specs=(P(("node", "local"), None), P(("node", "local"), None), P("local", "node")),
        check_vma=False,
    )
```

time: 550 us -> 69.1 us (0.13)
  waiting for transfers between devices: 434 us -> 0 us
  blocking collectives: 77.6 us -> 0 us
  Pallas kernels: 0 us -> 61.3 us
  between operations: 14.5 us -> 1.29 us
  matrix products: 10.4 us -> 0 us
    unnamed x4 -> x0, waiting for transfers between devices: 238 us -> none
    reduce_scatter x1 -> x0, waiting for transfers between devices: 118 us -> none  [body(): lax.psum_scatter(partial_sum, 'node', scatter_dimension=1, tiled=True)]
    all_gather x1 -> x0, waiting for transfers between devices: 78.4 us -> none  [body(): lax.all_gather(secondary, 'local', axis=0, tiled=True)]
    all_gather x2 -> x0, blocking collectives: 77.6 us -> none  [the longest x1 44.5 us: body(): lax.all_gather(scales, 'node', axis=1, tiled=True)]
    pallas_call x0 -> x1, Pallas kernels: none -> 61.3 us  [body(): pl.pallas_call(kernel, out_shape=(jax.ShapeDtypeStruct((frames, width), B...]
    dot_general x3 -> x0, matrix products: 10.4 us -> none  [the longest x1 3.68 us: body(): lax.dot_general(columns, masked, (((0,), (0,)), ((), ())), preferred_elem...]
    unnamed x8 -> x10, local copies, waits for them, and re-layouts: 11 us -> 6.2 us
  transfers between devices with their start and end apart: 3 -> 0, of which waited for: 3 -> 0; matrix products, arithmetic and copies ran while one was open for 3% -> 0% of each run, Pallas kernels for 0% -> 0%
where the time goes in v1:
time: 69.1 us; the launch traced here: 68.8 us
  Pallas kernels  61.3 us (89%)
  local copies, waits for them, and re-layouts  6.2 us (9%)
  between operations  1.29 us (2%)
    pallas_call x1, Pallas kernels, body(): pl.pallas_call(kernel, out_shape=(jax.ShapeDtypeStruct((frames, width), B...  61.3 us
    unnamed x10, local copies, waits for them, and re-layouts  6.2 us

profile of v1, /device:TPU:1, one launch (start us, length us, event | category | flops | bytes accessed | tf_op | source)
XLA Modules:
  0.0 68.8 jit_solution(12897843599309935754)
XLA Ops:
  1.3 0.7 %copy.8.scales_ref = bf16[24,1]{1,0:T(8,128)(2,1)S(1)} copy(bf16[24,1]{0,1:T(2,128)(2,1)} %param.8) | data formatting | bytes 96 | tf_op args[3]
  2.0 0.0 copy-start
  2.0 1.3 %copy-done = bf16[384,1536]{1,0:T(8,128)(2,1)S(1)} copy-done((bf16[384,1536]{1,0:T(8,128)(2,1)S(1)}, bf16[384,1536]{1,0:T(8,128)(2,1)}, u32[]{:S(2)}) %copy-start) | copy-done | bytes 1179672
  3.3 0.0 copy-start.1
  3.3 1.1 %copy-done.1 = bf16[384,768]{1,0:T(8,128)(2,1)S(1)} copy-done((bf16[384,768]{1,0:T(8,128)(2,1)S(1)}, bf16[384,768]{1,0:T(8,128)(2,1)}, u32[]{:S(2)}) %copy-start.1) | copy-done | bytes 589848
  4.4 0.0 copy-start.2
  4.4 0.7 %copy-done.2 = bf16[24,48]{1,0:T(8,128)(2,1)S(1)} copy-done((bf16[24,48]{1,0:T(8,128)(2,1)S(1)}, bf16[24,48]{1,0:T(8,128)(2,1)}, u32[]{:S(2)}) %copy-start.2) | copy-done | bytes 2328
  5.1 61.3 %shard_map.76 = (bf16[384,1536]{1,0:T(8,128)(2,1)S(1)}, bf16[384,768]{1,0:T(8,128)(2,1)S(1)}, f32[24,48]{1,0:T(8,128)S(1)}) custom-call(bf16[384,768]{1,0:T(8,128)(2,1)S(1)} %copy-done.1, bf16[384,1536]{1,0:T(8,128)(2,1)S(1)} %copy-done, bf16[24,48]{1,0:T(8,128)(2,1)S(1)} %copy-done.2, bf16[24,1]{1,0:T(8,128)(2,1)S(1)} %copy.8.scales_ref, s32[1]{0:T(128)S(6)} %copy.12.lengths_ref), custom_call_target="tpu_custom_call" | custom-call | tf_op jit(solution)/shard_map/pallas_call | solution.py:321
  66.4 1.0 %copy.13 = bf16[384,1536]{1,0:T(8,128)(2,1)} copy(bf16[384,1536]{1,0:T(8,128)(2,1)S(1)} %get-tuple-element.6) | data formatting | bytes 2359296
  67.4 0.8 %copy.14 = bf16[384,768]{1,0:T(8,128)(2,1)} copy(bf16[384,768]{1,0:T(8,128)(2,1)S(1)} %get-tuple-element.7) | data formatting | bytes 1179648
  68.2 0.6 copy.15
Async XLA Ops:
  2.0 1.3 %copy-start = (bf16[384,1536]{1,0:T(8,128)(2,1)S(1)}, bf16[384,1536]{1,0:T(8,128)(2,1)}, u32[]{:S(2)}) copy-start(bf16[384,1536]{1,0:T(8,128)(2,1)} %cotangent_hbm.1) | copy-start | bytes 3538948
  3.3 1.1 %copy-start.1 = (bf16[384,768]{1,0:T(8,128)(2,1)S(1)}, bf16[384,768]{1,0:T(8,128)(2,1)}, u32[]{:S(2)}) copy-start(bf16[384,768]{1,0:T(8,128)(2,1)} %context_hbm.1) | copy-start | bytes 1769476
  4.4 0.7 %copy-start.2 = (bf16[24,48]{1,0:T(8,128)(2,1)S(1)}, bf16[24,48]{1,0:T(8,128)(2,1)}, u32[]{:S(2)}) copy-start(bf16[24,48]{1,0:T(8,128)(2,1)} %codes_ref.1) | copy-start | bytes 6916

commit v2 on v1

v2 whole, which is shorter than its diff:
```python
import jax
import jax.numpy as jnp
from jax import lax
from jax.experimental import pallas as pl
from jax.experimental.pallas import tpu as pltpu
from jax.sharding import PartitionSpec as P

MESH = pl.DeviceIdType.MESH
F32, BF16 = jnp.float32, jnp.bfloat16
N = 8
RIGHT, LEFT = 0, 1
PIECES = 8


FAR = (4, 3, 5, 2, 6, 1, 7)


def kernel(
    context_hbm, cotangent_hbm, codes_hbm, scales_hbm, lengths,
    encoded, ctx_grad, weight_grad,
    context, cotangent, codes, scales, ctx_rows, cot_cols, enc_sum, cg_sum,
    grad, grad_in, weight, block,
    zsend, zbuf, ypack, ysend, ybuf,
    ring_out, ring_in, rsend, rbuf, xsend, xbuf,
    load_sem, z_s, z_r, y_s, y_r, ag_s, ag_r, fw_s, fw_r,
    pair_s, pair_r, ring_s, ring_r, ry_s, ry_r, rx_s, rx_r,
):
    node, local = lax.axis_index("node"), lax.axis_index("local")
    core, y, x_lo = node % 2, (node // 2) % N, node // (2 * N)
    x_hi, z = local // N, local % N
    x = x_hi * 2 + x_lo

    def at(cx, cy, cz, cc):
        return (((cx % 2) * N + cy) * 2 + cc, (cx // 2) * N + cz)

    def copy(src, dst, send, recv, target):
        return pltpu.make_async_remote_copy(
            src_ref=src, dst_ref=dst, send_sem=send, recv_sem=recv,
            device_id=target, device_id_type=MESH,
        )

    me, mate = at(x, y, z, core), at(x, y, z, 1 - core)

    barrier = pltpu.get_barrier_semaphore()

    def greet(target):
        pl.semaphore_signal(barrier, inc=1, device_id=target, device_id_type=MESH)

    for k in FAR:
        greet(at(x, y, (z + k) % N, core))
        for cc in range(2):
            greet(at(x, (y + k) % N, z, cc))
            greet(at((x + k) % N, y, z, cc))
    greet(mate)

    loads = [
        pltpu.make_async_copy(codes_hbm, codes, load_sem.at[2, 0]),
        pltpu.make_async_copy(scales_hbm, scales, load_sem.at[2, 1]),
    ]
    rows = context.shape[0] // PIECES
    for j, (src, dst) in enumerate(((context_hbm, context), (cotangent_hbm, cotangent))):
        for i in range(PIECES):
            spot = slice(i * rows, (i + 1) * rows)
            loads.append(pltpu.make_async_copy(src.at[spot], dst.at[spot], load_sem.at[j, i]))
    for c in loads:
        c.start()

    loads[0].wait()
    loads[1].wait()
    spread = lax.broadcasted_iota(jnp.int32, (24, 24), 0) == lax.broadcasted_iota(jnp.int32, (24, 24), 1)
    scale = jnp.sum(jnp.where(spread, scales[...].astype(F32), 0.0), axis=1, keepdims=True)
    zsend[0:24, 0:48] = (codes[...].astype(F32) * scale).astype(BF16)

    for c in loads[2 : 2 + PIECES]:
        c.wait()
    usable = lax.broadcasted_iota(jnp.int32, (context.shape[0], 1), 0) < lengths[0]
    context[...] = jnp.where(usable, context[...], jnp.zeros_like(context))
    for c in loads[2 + PIECES :]:
        c.wait()
    for h in range(2):
        cols = slice(h * 768, (h + 1) * 768)
        cot_cols[h] = jnp.where(usable, cotangent[:, cols], jnp.zeros((context.shape[0], 768), BF16))
    for i in range(2):
        for h in range(2):
            part = lax.dot_general(
                context[:, i * 384 : (i + 1) * 384], cot_cols[h],
                (((0,), (0,)), ((), ())), preferred_element_type=F32,
            )
            grad[h, 2 * i : 2 * i + 2] = part.reshape(2, N, 24, 768)

    pl.semaphore_wait(barrier, 1 + 5 * (N - 1))

    z_copies = [
        copy(zsend, zbuf.at[z], z_s.at[k], z_r.at[z], at(x, y, (z + k) % N, core)) for k in FAR
    ]
    for c in z_copies:
        c.start()
    zbuf[z] = zsend[...]

    pair = {}
    for k in FAR + (0,):
        pair[k] = copy(
            grad.at[1 - core, :, (z + k) % N], grad_in.at[k], pair_s.at[k], pair_r.at[k], mate
        )
        pair[k].start()

    paired = set()

    def own_part(k, q):
        if k not in paired:
            pair[k].wait_recv()
            paired.add(k)
        h, j = q // 2, q % 2
        cols = slice(j * 384, (j + 1) * 384)
        mine = grad[core, 2 * h : 2 * h + 2, (z + k) % N, :, cols]
        return (mine + grad_in[k, 2 * h : 2 * h + 2, :, cols]).reshape(48, 384)

    zn = (at(x, y, (z + 1) % N, core), at(x, y, (z + N - 1) % N, core))
    ring = {}

    def ring_send(way, d, q):
        part = own_part(d if way == RIGHT else N - d, q)
        if (way, d + 1, q) in ring:
            ring[way, d + 1, q].wait_recv()
            part = part + ring_in[way, d + 1, q].astype(F32)
        ring_out[way, d, q] = part.astype(BF16)
        c = copy(
            ring_out.at[way, d, q], ring_in.at[way, d, q], ring_s.at[way, d, q],
            ring_r.at[way, d, q], zn[way],
        )
        c.start()
        ring[way, d, q] = c

    def ring_long(d):
        for i in range(2):
            ring_send(RIGHT, d, i)
            ring_send(LEFT, d, 2 + i)

    def ring_short(d):
        for i in range(2):
            ring_send(RIGHT, d, 2 + i)
            ring_send(LEFT, d, i)

    ring_long(4)
    ring_short(3)

    for i in range(4):
        ctx_rows[i] = context[:, i * 192 : (i + 1) * 192]
    enc_sum[...] = jnp.zeros_like(enc_sum)
    cg_sum[...] = jnp.zeros_like(cg_sum)

    for k in range(1, N):
        s = (z + k) % N
        copy(zbuf.at[s], zbuf.at[s], z_s.at[k], z_r.at[s], me).wait_recv()
    for s in range(N):
        row, lane = (s % 4) * 24, (s // 4) * 64
        ypack[row : row + 24, lane : lane + 48] = zbuf[s, 0:24, 0:48].astype(F32)
    ysend[...] = ypack[...].astype(BF16)
    taker = y // 4
    slot = (y % 4) * 2 + core

    def y_copy(p, k):
        spot = slice(p * 48, (p + 1) * 48)
        return copy(
            ysend.at[spot], ybuf.at[slot, spot], y_s.at[p, k], y_r.at[p, slot],
            at(x, (y + k) % N, z, taker),
        )

    y_copies = [y_copy(p, k) for p in range(2) for k in FAR]

    @pl.when(taker == core)
    def _():
        ybuf[slot] = ysend[...]

    for p in range(2):
        for c in y_copies[p * 7 : p * 7 + 7]:
            c.start()

        @pl.when(taker != core)
        def _():
            y_copy(p, 0).start()

    ring_long(3)
    ring_short(2)
    ring_long(2)

    def place(k, q, cc):
        cx = (x + k + N) % N
        row = pl.multiple_of((cx // 2) * 192 + q * 48, 16)
        col = pl.multiple_of((cx % 2) * 768 + cc * 384, 128)
        return weight.at[pl.ds(row, 48), pl.ds(col, 384)]

    xn = (at((x + 1) % N, y, z, core), at((x + N - 1) % N, y, z, core))
    gather, forward = {}, []

    def shared(way, s, q, cc):
        spot = place(-s if way == RIGHT else s, q, cc)
        return copy(spot, spot, fw_s.at[way, s, q], fw_r.at[way, s, q], mate)

    def share(way, s, q):
        shared(way, s, q, core).start()
        forward.append((way, s, q))

    def gather_send(s, q):
        for way in (RIGHT, LEFT):
            if s > 1 and (way, s - 1, q) not in gather:
                continue
            if s > 1:
                gather[way, s - 1, q].wait_recv()
            if s <= 3 or (s == 4 and (q < 2) == (way == RIGHT)):
                spot = place(1 - s if way == RIGHT else s - 1, q, core)
                c = copy(spot, spot, ag_s.at[way, s, q], ag_r.at[way, s, q], xn[way])
                c.start()
                gather[way, s, q] = c
        for way in (RIGHT, LEFT):
            if (s == 1 and way == RIGHT) or (s > 1 and (way, s - 1, q) in gather):
                share(way, s - 1, q)

    def products(k, pieces):
        for way, s, q in pieces:
            shared(way, s, q, 1 - core).wait_recv()
        cx = (x + k + N) % N
        row = pl.multiple_of((cx // 2) * 192, 16)
        col = pl.multiple_of((cx % 2) * 768, 128)
        entries = weight[pl.ds(row, 192), pl.ds(col, 768)]
        enc_sum[cx % 2] += jnp.dot(ctx_rows[cx // 2], entries, preferred_element_type=F32)
        cg_sum[cx // 2] += lax.dot_general(
            cot_cols[cx % 2], entries, (((1,), (1,)), ((), ())), preferred_element_type=F32
        )

    def products_at(s):
        if s == 0:
            products(0, [(RIGHT, 0, q) for q in range(4)])
        elif s == 4:
            products(4, [(RIGHT if q < 2 else LEFT, 4, q) for q in range(4)])
        else:
            products(-s, [(RIGHT, s, q) for q in range(4)])
            products(s, [(LEFT, s, q) for q in range(4)])

    def assemble(p):
        spot = slice(p * 48, (p + 1) * 48)
        for s in range(N):
            @pl.when((4 * core + s // 2 != y) | (core != s % 2))
            def _():
                piece = ybuf.at[s, spot]
                copy(piece, piece, y_s.at[p, 0], y_r.at[p, s], me).wait_recv()

            cols = slice(s * 48, (s + 1) * 48)
            block[p * 48 : (p + 1) * 48, cols] = ybuf[s, spot, 0:48].astype(F32)
            block[96 + p * 48 : 96 + (p + 1) * 48, cols] = ybuf[s, spot, 64:112].astype(F32)
        for q in (p, p + 2):
            place(0, q, core)[...] = block[q * 48 : (q + 1) * 48, :].astype(BF16)
            gather_send(1, q)

    assemble(0)
    ring_short(1)
    assemble(1)
    ring_long(1)
    for q in (0, 2):
        gather_send(2, q)
    products_at(0)
    for q in (1, 3):
        gather_send(2, q)

    def ry_copy(h, k):
        spot = slice(h * 48, (h + 1) * 48)
        return copy(
            rsend.at[(y + k) % N, spot], rbuf.at[y, spot], ry_s.at[h, k], ry_r.at[h, y],
            at(x, (y + k) % N, z, core),
        )

    ry_copies = [ry_copy(h, k) for h in range(2) for k in FAR]
    for h in range(2):
        for j in range(2):
            q = 2 * h + j
            ring[RIGHT, 1, q].wait_recv()
            ring[LEFT, 1, q].wait_recv()
            total = own_part(0, q) + ring_in[RIGHT, 1, q].astype(F32) + ring_in[LEFT, 1, q].astype(F32)
            for k in range(4):
                rsend[4 * j + k, h * 48 : (h + 1) * 48, 0:96] = total[:, k * 96 : (k + 1) * 96].astype(BF16)
        for c in ry_copies[h * 7 : h * 7 + 7]:
            c.start()

    for q in (0, 2):
        gather_send(3, q)
    products_at(1)
    for q in (1, 3):
        gather_send(3, q)
    for q in (0, 2):
        gather_send(4, q)

    def rx_copy(i, cc):
        return copy(
            xsend.at[i, cc], xbuf.at[x], rx_s.at[2 * i + cc], rx_r.at[x], at(i * 2 + core, y, z, cc)
        )

    def stays(i, cc):
        return (x_hi == i) & (x_lo == core) & (core == cc)

    for h in range(2):
        spot = slice(h * 48, (h + 1) * 48)
        summed = rsend[y, spot].astype(F32)
        for k in range(1, N):
            s = (y + k) % N
            piece = rbuf.at[s, spot]
            copy(piece, piece, ry_s.at[h, k], ry_r.at[h, s], me).wait_recv()
            summed = summed + rbuf[s, spot].astype(F32)
        for i in range(2):
            for cc in range(2):
                for r in range(3):
                    rows = slice(i * 24 + r * 8, i * 24 + r * 8 + 8)
                    xsend[2 * h + i, cc, :, r * 64 : r * 64 + 48] = summed[rows, cc * 48 : (cc + 1) * 48]
        for i in (2 * h, 2 * h + 1):
            for cc in range(2):
                @pl.when(jnp.logical_not(stays(i, cc)))
                def _():
                    rx_copy(i, cc).start()

                @pl.when(stays(i, cc))
                def _():
                    xbuf[x] = xsend[i, cc]

    for q in (1, 3):
        gather_send(4, q)
    products_at(2)
    for q in range(4):
        gather_send(5, q)
    products_at(3)
    products_at(4)
    for h in range(2):
        encoded[:, h * 768 : (h + 1) * 768] = enc_sum[h].astype(BF16)
    for i in range(4):
        ctx_grad[:, i * 192 : (i + 1) * 192] = cg_sum[i].astype(BF16)

    for k in range(1, N):
        s = (x + k) % N
        copy(xbuf.at[s], xbuf.at[s], rx_s.at[0], rx_r.at[s], me).wait_recv()

    @pl.when(x_lo != core)
    def _():
        copy(xbuf.at[x], xbuf.at[x], rx_s.at[0], rx_r.at[x], me).wait_recv()

    last = xbuf[0]
    for s in range(1, N):
        last = last + xbuf[s]
    for r in range(3):
        weight_grad[r * 8 : r * 8 + 8, :] = last[:, r * 64 : r * 64 + 48] * (1.0 / 1024)

    for c in z_copies + y_copies + ry_copies:
        c.wait_send()

    @pl.when(taker != core)
    def _():
        for p in range(2):
            y_copy(p, 0).wait_send()

    for i in range(4):
        for cc in range(2):
            @pl.when(jnp.logical_not(stays(i, cc)))
            def _():
                rx_copy(i, cc).wait_send()

    for c in list(pair.values()) + list(ring.values()) + list(gather.values()):
        c.wait_send()
    for way, s, q in forward:
        shared(way, s, q, core).wait_send()


def store(encoded, ctx_grad, weight_grad, encoded_hbm, ctx_grad_hbm, weight_grad_hbm, sems):
    copies = [pltpu.make_async_copy(weight_grad, weight_grad_hbm, sems.at[2, 0])]
    rows = encoded.shape[0] // PIECES
    for i in range(PIECES):
        spot = slice(i * rows, (i + 1) * rows)
        copies.append(pltpu.make_async_copy(encoded.at[spot], encoded_hbm.at[spot], sems.at[0, i]))
        copies.append(pltpu.make_async_copy(ctx_grad.at[spot], ctx_grad_hbm.at[spot], sems.at[1, i]))
    for c in copies:
        c.start()
    for c in copies:
        c.wait()


def body(context, cotangent, codes, scales, lengths):
    frames, hrows = context.shape
    width = cotangent.shape[1]
    vmem = pl.BlockSpec(memory_space=pltpu.VMEM)
    hbm = pl.BlockSpec(memory_space=pltpu.HBM)
    dma = pltpu.SemaphoreType.DMA
    shape = jax.ShapeDtypeStruct
    operands = [
        pltpu.with_memory_space_constraint(a, pltpu.HBM)
        for a in (context, cotangent, codes, scales.T)
    ]
    held = pl.pallas_call(
        kernel,
        out_shape=(
            pltpu.VMEM((frames, width), BF16), pltpu.VMEM((frames, hrows), BF16),
            pltpu.VMEM(codes.shape, F32),
        ),
        in_specs=[hbm] * 4 + [pl.BlockSpec(memory_space=pltpu.SMEM)],
        out_specs=(vmem, vmem, vmem),
        scratch_shapes=[
            pltpu.VMEM((frames, hrows), BF16),
            pltpu.VMEM((frames, width), BF16),
            pltpu.VMEM(codes.shape, BF16),
            pltpu.VMEM((1, codes.shape[0]), BF16),
            pltpu.VMEM((4, frames, hrows // 4), BF16),
            pltpu.VMEM((2, frames, width // 2), BF16),
            pltpu.VMEM((2, frames, width // 2), F32),
            pltpu.VMEM((4, frames, hrows // 4), F32),
            pltpu.VMEM((2, 4, N, 24, width // 2), F32),
            pltpu.VMEM((N, 4, 24, width // 2), F32),
            pltpu.VMEM((hrows, width), BF16),
            pltpu.VMEM((192, 384), F32),
            pltpu.VMEM((32, 128), BF16),
            pltpu.VMEM((N, 32, 128), BF16),
            pltpu.VMEM((96, 128), F32),
            pltpu.VMEM((96, 128), BF16),
            pltpu.VMEM((N, 96, 128), BF16),
            pltpu.VMEM((2, 5, 4, 48, 384), BF16),
            pltpu.VMEM((2, 5, 4, 48, 384), BF16),
            pltpu.VMEM((N, 96, 128), BF16),
            pltpu.VMEM((N, 96, 128), BF16),
            pltpu.VMEM((4, 2, 8, 256), F32),
            pltpu.VMEM((N, 8, 256), F32),
            dma((3, PIECES)),
            dma((N,)), dma((N,)),
            dma((2, N)), dma((2, N)),
            dma((2, 5, 4)), dma((2, 5, 4)),
            dma((2, 5, 4)), dma((2, 5, 4)),
            dma((N,)), dma((N,)),
            dma((2, 5, 4)), dma((2, 5, 4)),
            dma((2, N)), dma((2, N)),
            dma((N,)), dma((N,)),
        ],
        compiler_params=pltpu.CompilerParams(
            collective_id=0, has_side_effects=True, vmem_limit_bytes=40 * 2**20
        ),
    )(*operands, lengths)
    return pl.pallas_call(
        store,
        out_shape=(
            shape((frames, width), BF16), shape((frames, hrows), BF16), shape(codes.shape, F32),
        ),
        in_specs=[vmem] * 3,
        out_specs=(hbm,) * 3,
        scratch_shapes=[dma((3, PIECES))],
    )(*(pltpu.with_memory_space_constraint(a, pltpu.VMEM) for a in held))


def solution(mesh):
    return jax.shard_map(
        body,
        mesh=mesh,
        in_specs=(
            P(("node", "local"), None),
            P(("node", "local"), None),
            P("local", "node"),
            P("local", "node"),
            P(("node", "local")),
        ),
        out_specs=(P(("node", "local"), None), P(("node", "local"), None), P("local", "node")),
        check_vma=False,
    )
```

time: 69.1 us -> 59.1 us (0.86)
  local copies, waits for them, and re-layouts: 6.2 us -> 0 us
  Pallas kernels: 61.3 us -> 57.6 us
    unnamed x10 -> x0, local copies, waits for them, and re-layouts: 6.2 us -> none
    pallas_call x1 -> x2, Pallas kernels: 61.3 us -> 57.6 us  [the longest x1 56.2 us: body(): pl.pallas_call(kernel, out_shape=(pltpu.VMEM((frames, width), BF16), pltp...]
where the time goes in v2:
time: 59.1 us; the launch traced here: 58.9 us
  Pallas kernels  57.6 us (97%)
  between operations  1.29 us (2%)
    pallas_call x1, Pallas kernels, body(): pl.pallas_call(kernel, out_shape=(pltpu.VMEM((frames, width), BF16), pltp...  56.2 us
    pallas_call x1, Pallas kernels, body(): pl.pallas_call(store, out_shape=(shape((frames, width), BF16), shape((fra...  1.41 us

profile of v2, /device:TPU:1, one launch (start us, length us, event | category | flops | bytes accessed | tf_op | source)
XLA Modules:
  0.0 58.9 jit_solution(7703986940513155121)
XLA Ops:
  1.3 56.2 %shard_map.76 = (bf16[384,1536]{1,0:T(8,128)(2,1)S(1)}, bf16[384,768]{1,0:T(8,128)(2,1)S(1)}, f32[24,48]{1,0:T(8,128)S(1)}) custom-call(bf16[384,768]{1,0:T(8,128)(2,1)} %context_hbm.1, bf16[384,1536]{1,0:T(8,128)(2,1)} %cotangent_hbm.1, bf16[24,48]{1,0:T(8,128)(2,1)} %codes_hbm.1, bf16[1,24]{1,0:T(2,128)(2,1)} %bitcast.1, s32[1]{0:T(128)S(6)} %copy.8.lengths), custom_call_target="tpu_custom_call" | custom-call | tf_op jit(solution)/shard_map/pallas_call | solution.py:393
  57.5 1.4 %shard_map.77 = (bf16[384,1536]{1,0:T(8,128)(2,1)}, bf16[384,768]{1,0:T(8,128)(2,1)}, f32[24,48]{1,0:T(8,128)}) custom-call(bf16[384,1536]{1,0:T(8,128)(2,1)S(1)} %get-tuple-element.6.encoded, bf16[384,768]{1,0:T(8,128)(2,1)S(1)} %get-tuple-element.7.ctx_grad, f32[24,48]{1,0:T(8,128)S(1)} %get-tuple-element.8.weight_grad), custom_call_target="tpu_custom_call" | custom-call | tf_op jit(solution)/shard_map/pallas_call | solution.py:439

commit v3 on v2

--- a/solution.py
+++ b/solution.py
@@ -18,7 +18,7 @@
 def kernel(
     context_hbm, cotangent_hbm, codes_hbm, scales_hbm, lengths,
     encoded, ctx_grad, weight_grad,
-    context, cotangent, codes, scales, ctx_rows, cot_cols, enc_sum, cg_sum,
+    context, cotangent, codes, scales, ctx_turned, ctx_rows, cot_cols, enc_sum, cg_sum,
     grad, grad_in, weight, block,
     zsend, zbuf, ypack, ysend, ybuf,
     ring_out, ring_in, rsend, rbuf, xsend, xbuf,
@@ -75,19 +75,18 @@
         c.wait()
     usable = lax.broadcasted_iota(jnp.int32, (context.shape[0], 1), 0) < lengths[0]
     context[...] = jnp.where(usable, context[...], jnp.zeros_like(context))
+    ctx_turned[...] = context[...].T
+
     for c in loads[2 + PIECES :]:
         c.wait()
-    for h in range(2):
-        cols = slice(h * 768, (h + 1) * 768)
-        cot_cols[h] = jnp.where(usable, cotangent[:, cols], jnp.zeros((context.shape[0], 768), BF16))
-    for i in range(2):
-        for h in range(2):
-            part = lax.dot_general(
-                context[:, i * 384 : (i + 1) * 384], cot_cols[h],
-                (((0,), (0,)), ((), ())), preferred_element_type=F32,
-            )
+
+    def own_gradient(h):
+        entries = cotangent[:, pl.ds(pl.multiple_of(h * 768, 128), 768)]
+        for i in range(2):
+            part = jnp.dot(ctx_turned[i * 384 : (i + 1) * 384], entries, preferred_element_type=F32)
             grad[h, 2 * i : 2 * i + 2] = part.reshape(2, N, 24, 768)
 
+    own_gradient(1 - core)
     pl.semaphore_wait(barrier, 1 + 5 * (N - 1))
 
     z_copies = [
@@ -103,6 +102,7 @@
             grad.at[1 - core, :, (z + k) % N], grad_in.at[k], pair_s.at[k], pair_r.at[k], mate
         )
         pair[k].start()
+    own_gradient(core)
 
     paired = set()
 
@@ -141,21 +141,6 @@
             ring_send(RIGHT, d, 2 + i)
             ring_send(LEFT, d, i)
 
-    ring_long(4)
-    ring_short(3)
-
-    for i in range(4):
-        ctx_rows[i] = context[:, i * 192 : (i + 1) * 192]
-    enc_sum[...] = jnp.zeros_like(enc_sum)
-    cg_sum[...] = jnp.zeros_like(cg_sum)
-
-    for k in range(1, N):
-        s = (z + k) % N
-        copy(zbuf.at[s], zbuf.at[s], z_s.at[k], z_r.at[s], me).wait_recv()
-    for s in range(N):
-        row, lane = (s % 4) * 24, (s // 4) * 64
-        ypack[row : row + 24, lane : lane + 48] = zbuf[s, 0:24, 0:48].astype(F32)
-    ysend[...] = ypack[...].astype(BF16)
     taker = y // 4
     slot = (y % 4) * 2 + core
 
@@ -168,21 +153,35 @@
 
     y_copies = [y_copy(p, k) for p in range(2) for k in FAR]
 
-    @pl.when(taker == core)
-    def _():
-        ybuf[slot] = ysend[...]
-
-    for p in range(2):
-        for c in y_copies[p * 7 : p * 7 + 7]:
-            c.start()
-
-        @pl.when(taker != core)
+    def weight_rows():
+        for k in range(1, N):
+            s = (z + k) % N
+            copy(zbuf.at[s], zbuf.at[s], z_s.at[k], z_r.at[s], me).wait_recv()
+        for s in range(N):
+            row, lane = (s % 4) * 24, (s // 4) * 64
+            ypack[row : row + 24, lane : lane + 48] = zbuf[s, 0:24, 0:48].astype(F32)
+        ysend[...] = ypack[...].astype(BF16)
+
+        @pl.when(taker == core)
         def _():
-            y_copy(p, 0).start()
-
-    ring_long(3)
-    ring_short(2)
-    ring_long(2)
+            ybuf[slot] = ysend[...]
+
+        for p in range(2):
+            for c in y_copies[p * 7 : p * 7 + 7]:
+                c.start()
+
+            @pl.when(taker != core)
+            def _():
+                y_copy(p, 0).start()
+
+    def prepare():
+        for i in range(4):
+            ctx_rows[i] = context[:, i * 192 : (i + 1) * 192]
+        for h in range(2):
+            cols = slice(h * 768, (h + 1) * 768)
+            cot_cols[h] = jnp.where(usable, cotangent[:, cols], jnp.zeros((context.shape[0], 768), BF16))
+        enc_sum[...] = jnp.zeros_like(enc_sum)
+        cg_sum[...] = jnp.zeros_like(cg_sum)
 
     def place(k, q, cc):
         cx = (x + k + N) % N
@@ -252,15 +251,9 @@
             place(0, q, core)[...] = block[q * 48 : (q + 1) * 48, :].astype(BF16)
             gather_send(1, q)
 
-    assemble(0)
-    ring_short(1)
-    assemble(1)
-    ring_long(1)
-    for q in (0, 2):
-        gather_send(2, q)
-    products_at(0)
-    for q in (1, 3):
-        gather_send(2, q)
+    def gather_both(s, first):
+        for q in (first, first + 2):
+            gather_send(s, q)
 
     def ry_copy(h, k):
         spot = slice(h * 48, (h + 1) * 48)
@@ -270,7 +263,7 @@
         )
 
     ry_copies = [ry_copy(h, k) for h in range(2) for k in FAR]
-    for h in range(2):
+    def segment(h):
         for j in range(2):
             q = 2 * h + j
             ring[RIGHT, 1, q].wait_recv()
@@ -281,14 +274,6 @@
         for c in ry_copies[h * 7 : h * 7 + 7]:
             c.start()
 
-    for q in (0, 2):
-        gather_send(3, q)
-    products_at(1)
-    for q in (1, 3):
-        gather_send(3, q)
-    for q in (0, 2):
-        gather_send(4, q)
-
     def rx_copy(i, cc):
         return copy(
             xsend.at[i, cc], xbuf.at[x], rx_s.at[2 * i + cc], rx_r.at[x], at(i * 2 + core, y, z, cc)
@@ -297,7 +282,7 @@
     def stays(i, cc):
         return (x_hi == i) & (x_lo == core) & (core == cc)
 
-    for h in range(2):
+    def summed_over_y(h):
         spot = slice(h * 48, (h + 1) * 48)
         summed = rsend[y, spot].astype(F32)
         for k in range(1, N):
@@ -320,17 +305,45 @@
                 def _():
                     xbuf[x] = xsend[i, cc]
 
-    for q in (1, 3):
-        gather_send(4, q)
+    def finish(far):
+        half = x_lo if far else 1 - x_lo
+        col = pl.multiple_of(half * 768, 128)
+        encoded[:, pl.ds(col, 768)] = enc_sum[half].astype(BF16)
+        if far:
+            for i in range(4):
+                ctx_grad[:, i * 192 : (i + 1) * 192] = cg_sum[i].astype(BF16)
+
+    ring_long(4)
+    ring_short(3)
+    prepare()
+    weight_rows()
+    ring_long(3)
+    ring_short(2)
+    ring_long(2)
+    assemble(0)
+    ring_short(1)
+    assemble(1)
+    ring_long(1)
+    gather_both(2, 0)
+    products_at(0)
+    segment(0)
+    segment(1)
+    gather_both(2, 1)
+    gather_both(3, 0)
+    products_at(1)
+    gather_both(3, 1)
+    gather_both(4, 0)
+    summed_over_y(0)
+    summed_over_y(1)
+    gather_both(4, 1)
     products_at(2)
-    for q in range(4):
-        gather_send(5, q)
     products_at(3)
+    finish(False)
+    gather_both(5, 0)
+    gather_both(5, 1)
     products_at(4)
-    for h in range(2):
-        encoded[:, h * 768 : (h + 1) * 768] = enc_sum[h].astype(BF16)
-    for i in range(4):
-        ctx_grad[:, i * 192 : (i + 1) * 192] = cg_sum[i].astype(BF16)
+    finish(True)
+
 
     for k in range(1, N):
         s = (x + k) % N
@@ -403,6 +416,7 @@
             pltpu.VMEM((frames, width), BF16),
             pltpu.VMEM(codes.shape, BF16),
             pltpu.VMEM((1, codes.shape[0]), BF16),
+            pltpu.VMEM((hrows, frames), BF16),
             pltpu.VMEM((4, frames, hrows // 4), BF16),
             pltpu.VMEM((2, frames, width // 2), BF16),
             pltpu.VMEM((2, frames, width // 2), F32),

time: 59.1 us -> 58.3 us (0.986)
  Pallas kernels: 57.6 us -> 56.8 us
    pallas_call x1, Pallas kernels: 56.2 us -> 55.4 us  [body(): pl.pallas_call(kernel, out_shape=(pltpu.VMEM((frames, width), BF16), pltp...]
where the time goes in v3:
time: 58.3 us; the launch traced here: 58.1 us
  Pallas kernels  56.8 us (97%)
  between operations  1.29 us (2%)
    pallas_call x1, Pallas kernels, body(): pl.pallas_call(kernel, out_shape=(pltpu.VMEM((frames, width), BF16), pltp...  55.4 us
    pallas_call x1, Pallas kernels, body(): pl.pallas_call(store, out_shape=(shape((frames, width), BF16), shape((fra...  1.41 us

profile of v3, /device:TPU:1, one launch (start us, length us, event | category | flops | bytes accessed | tf_op | source)
XLA Modules:
  0.0 58.1 jit_solution(6534081979773813943)
XLA Ops:
  1.3 55.4 %shard_map.76 = (bf16[384,1536]{1,0:T(8,128)(2,1)S(1)}, bf16[384,768]{1,0:T(8,128)(2,1)S(1)}, f32[24,48]{1,0:T(8,128)S(1)}) custom-call(bf16[384,768]{1,0:T(8,128)(2,1)} %context_hbm.1, bf16[384,1536]{1,0:T(8,128)(2,1)} %cotangent_hbm.1, bf16[24,48]{1,0:T(8,128)(2,1)} %codes_hbm.1, bf16[1,24]{1,0:T(2,128)(2,1)} %bitcast.1, s32[1]{0:T(128)S(6)} %copy.8.lengths), custom_call_target="tpu_custom_call" | custom-call | tf_op jit(solution)/shard_map/pallas_call | solution.py:406
  56.7 1.4 %shard_map.77 = (bf16[384,1536]{1,0:T(8,128)(2,1)}, bf16[384,768]{1,0:T(8,128)(2,1)}, f32[24,48]{1,0:T(8,128)}) custom-call(bf16[384,1536]{1,0:T(8,128)(2,1)S(1)} %get-tuple-element.6.encoded, bf16[384,768]{1,0:T(8,128)(2,1)S(1)} %get-tuple-element.7.ctx_grad, f32[24,48]{1,0:T(8,128)S(1)} %get-tuple-element.8.weight_grad), custom_call_target="tpu_custom_call" | custom-call | tf_op jit(solution)/shard_map/pallas_call | solution.py:453

commit v4 on v3

--- a/solution.py
+++ b/solution.py
@@ -16,9 +16,9 @@
 
 
 def kernel(
-    context_hbm, cotangent_hbm, codes_hbm, scales_hbm, lengths,
+    context_hbm, cotangent_hbm, codes_hbm, scales_hbm, lengths_hbm,
     encoded, ctx_grad, weight_grad,
-    context, cotangent, codes, scales, ctx_turned, ctx_rows, cot_cols, enc_sum, cg_sum,
+    context, cotangent, codes, scales, lengths, ctx_turned, ctx_rows, cot_cols, enc_sum, cg_sum,
     grad, grad_in, weight, block,
     zsend, zbuf, ypack, ysend, ybuf,
     ring_out, ring_in, rsend, rbuf, xsend, xbuf,
@@ -56,6 +56,7 @@
     loads = [
         pltpu.make_async_copy(codes_hbm, codes, load_sem.at[2, 0]),
         pltpu.make_async_copy(scales_hbm, scales, load_sem.at[2, 1]),
+        pltpu.make_async_copy(lengths_hbm, lengths, load_sem.at[2, 2]),
     ]
     rows = context.shape[0] // PIECES
     for j, (src, dst) in enumerate(((context_hbm, context), (cotangent_hbm, cotangent))):
@@ -71,13 +72,13 @@
     scale = jnp.sum(jnp.where(spread, scales[...].astype(F32), 0.0), axis=1, keepdims=True)
     zsend[0:24, 0:48] = (codes[...].astype(F32) * scale).astype(BF16)
 
-    for c in loads[2 : 2 + PIECES]:
+    for c in loads[2 : 3 + PIECES]:
         c.wait()
-    usable = lax.broadcasted_iota(jnp.int32, (context.shape[0], 1), 0) < lengths[0]
+    usable = lax.broadcasted_iota(jnp.int32, (context.shape[0], 1), 0) < lengths[0, 0]
     context[...] = jnp.where(usable, context[...], jnp.zeros_like(context))
     ctx_turned[...] = context[...].T
 
-    for c in loads[2 + PIECES :]:
+    for c in loads[3 + PIECES :]:
         c.wait()
 
     def own_gradient(h):
@@ -409,13 +410,14 @@
             pltpu.VMEM((frames, width), BF16), pltpu.VMEM((frames, hrows), BF16),
             pltpu.VMEM(codes.shape, F32),
         ),
-        in_specs=[hbm] * 4 + [pl.BlockSpec(memory_space=pltpu.SMEM)],
+        in_specs=[hbm] * 5,
         out_specs=(vmem, vmem, vmem),
         scratch_shapes=[
             pltpu.VMEM((frames, hrows), BF16),
             pltpu.VMEM((frames, width), BF16),
             pltpu.VMEM(codes.shape, BF16),
             pltpu.VMEM((1, codes.shape[0]), BF16),
+            pltpu.SMEM((1, 1), jnp.int32),
             pltpu.VMEM((hrows, frames), BF16),
             pltpu.VMEM((4, frames, hrows // 4), BF16),
             pltpu.VMEM((2, frames, width // 2), BF16),
@@ -449,7 +451,7 @@
         compiler_params=pltpu.CompilerParams(
             collective_id=0, has_side_effects=True, vmem_limit_bytes=40 * 2**20
         ),
-    )(*operands, lengths)
+    )(*operands, lengths.reshape(1, 1))
     return pl.pallas_call(
         store,
         out_shape=(

time: 58.3 us -> 58.3 us (level)
  no operation moved by 1% of the time
where the time goes in v4:
time: 58.3 us; the launch traced here: 58.1 us
  Pallas kernels  56.8 us (97%)
  between operations  1.29 us (2%)
    pallas_call x1, Pallas kernels, body(): pl.pallas_call(kernel, out_shape=(pltpu.VMEM((frames, width), BF16), pltp...  55.4 us
    pallas_call x1, Pallas kernels, body(): pl.pallas_call(store, out_shape=(shape((frames, width), BF16), shape((fra...  1.41 us

profile of v4, /device:TPU:1, one launch (start us, length us, event | category | flops | bytes accessed | tf_op | source)
XLA Modules:
  0.0 58.1 jit_solution(6142148513839575079)
XLA Ops:
  1.3 55.4 %shard_map.76 = (bf16[384,1536]{1,0:T(8,128)(2,1)S(1)}, bf16[384,768]{1,0:T(8,128)(2,1)S(1)}, f32[24,48]{1,0:T(8,128)S(1)}) custom-call(bf16[384,768]{1,0:T(8,128)(2,1)} %context_hbm.1, bf16[384,1536]{1,0:T(8,128)(2,1)} %cotangent_hbm.1, bf16[24,48]{1,0:T(8,128)(2,1)} %codes_hbm.1, bf16[1,24]{1,0:T(2,128)(2,1)} %bitcast.3, s32[1,1]{1,0:T(1,128)} %bitcast.2.lengths_hbm), custom_call_target="tpu_custom_call" | custom-call | tf_op jit(solution)/shard_map/pallas_call | solution.py:407
  56.7 1.4 %shard_map.77 = (bf16[384,1536]{1,0:T(8,128)(2,1)}, bf16[384,768]{1,0:T(8,128)(2,1)}, f32[24,48]{1,0:T(8,128)}) custom-call(bf16[384,1536]{1,0:T(8,128)(2,1)S(1)} %get-tuple-element.6.encoded, bf16[384,768]{1,0:T(8,128)(2,1)S(1)} %get-tuple-element.7.ctx_grad, f32[24,48]{1,0:T(8,128)S(1)} %get-tuple-element.8.weight_grad), custom_call_target="tpu_custom_call" | custom-call | tf_op jit(solution)/shard_map/pallas_call | solution.py:455
